TPU v7x, 128 devices: a whole 4x4x4 slice. The times are simulated.
128 devices in a mesh: rep: 4 (over y), shard: 32 (over x, z, core).
Axes of the slice: x: 4, y: 4, z: 4, core: 2. Of those that a mesh axis runs over, the one named last changes fastest.
Arguments:
- embed_table: bfloat16 [262144, 128], P('shard'), may hold values from -6 to 6
- row_ids: int32 [128, 8192], P(('rep', 'shard')), may hold values from 0 to 1023
- row_owner: int32 [128, 8192, 1], P(('rep', 'shard')), may hold values from 0 to 31; in each aligned block of 8192 rows (0 to 8191, 8192 to 16383, ..., all dimensions but the last counted through in order) at most 512 rows name the same one
- lengths: int32 [128, 1024], P(('rep', 'shard')), may hold values from 1 to 200, 8192 in all within a row
- feature_slot: int32 [32, 8], replicated, may hold values from 0 to 7, each once within a row
- labels: int32 [16384], P(('rep', 'shard')), may hold values 0 or 1
- norm_gain: float32 [1024], replicated, may hold values from 0.1 to 1.9
- cross_weight: bfloat16 [3, 1024, 1024], replicated, may hold values from -0.1875 to 0.1875
- cross_bias: float32 [3, 1024], replicated, may hold values from -3 to 3
- deep_weight: bfloat16 [3, 1024, 1024], replicated, may hold values from -0.1875 to 0.1875
- deep_bias: float32 [3, 1024], replicated, may hold values from -3 to 3
- out_weight: float32 [1024], replicated, may hold values from -0.1875 to 0.1875
Outputs:
- row_grad: float32 [262144, 128], P('shard')
- first_grad: float32 [1024, 1024], replicated
- logits: float32 [16384], P(('rep', 'shard'))
Inputs may be any that keep to these rules, and one draw needn't show every extreme that they name: `row_owner`: among one device's ids, at most 512 have the same owner, and in every draw some device sends exactly 512 to some owner. Each device's 1024 lengths sum to 8192; the largest is 200. `feature_slot`: each row holds each of 0 to 7 once.
All inputs are finite; a program needn't handle non-finite values. No bound on the sum of `labels` on one device may be relied on, other than what follows from the above.
Results may differ from a plain program's by a relative error of at most 0.035.
Values may be sent and summed in bfloat16 or wider, within the bound.
No kernel may reach another device: no remote copies, remote signals or barrier semaphores. Data moves between devices by JAX's collectives and lax.ppermute only.
A program may use at most 128 MiB of HBM per device.

v0:
```python
import functools

import jax
import jax.numpy as jnp
import numpy as np
from jax import lax
from jax.experimental import pallas as pl
from jax.experimental.pallas import tpu as pltpu
from jax.sharding import PartitionSpec as P

BF = jnp.bfloat16
F32 = jnp.float32
I32 = jnp.int32
OWNERS = 32
FEATS = 8
KEYS = OWNERS * FEATS
CAP = 512
VOC = 1024
ROWS = FEATS * VOC
EMB = 128
BAGS = 1024
SAMPLES = 128
WIDTH = FEATS * EMB
IDS = 8192
REPS = 4
CORES = 2
CHIPS = OWNERS // CORES
PAIR = FEATS // REPS
LANES = 256
IDROWS = IDS // LANES
ACCS = 16
POOLED = 16
GROUP = 4
LISTED = CAP + 64
LISTS = 16
SOURCES = GROUP * REPS * PAIR * SAMPLES
SHIFT = 13
EARLY = 128
VMEM = 62 * 1024 * 1024

NT = (((1,), (1,)), ((), ()))
TN = (((0,), (0,)), ((), ()))


def dot(a, b, dims=(((1,), (0,)), ((), ()))):
    return lax.dot_general(a, b, dims, preferred_element_type=F32)


def iota(shape, dim):
    return lax.broadcasted_iota(I32, shape, dim)


def onehot(cond):
    return jnp.where(cond, 1.0, 0.0).astype(BF)


def index_kernel(
    ids_in, owner_in, len_in, slot_ref, out_ref, send_ref, ids_ref, owner_ref, len_ref, bag_ref, key_ref
):
    for r in range(IDROWS):
        ids_ref[r : r + 1, :] = ids_in[:, r * LANES : (r + 1) * LANES]
        owner_ref[r : r + 1, :] = owner_in[:, r * LANES : (r + 1) * LANES]
    for r in range(BAGS // 128):
        len_ref[r : r + 1, :] = len_in[:, r * 128 : (r + 1) * 128]
    lens = len_ref[...].astype(F32).astype(BF)
    incl128 = onehot(iota((128, 128), 0) <= iota((128, 128), 1))
    within = dot(lens, incl128)
    total = jnp.broadcast_to(within[:, 127:128], (8, 128))
    high = jnp.floor(total * (1.0 / 256.0))
    low = total - high * 256.0
    below8 = onehot(iota((8, 8), 1) < iota((8, 8), 0))
    before = dot(below8, high.astype(BF)) * 256.0 + dot(below8, low.astype(BF))
    start = (within + before).astype(I32) - len_ref[...]
    start_hi = start >> 8
    start_lo = start & 255
    marks = jnp.zeros((IDROWS, LANES), F32)
    for r in range(8):
        a = onehot(iota((IDROWS, 128), 0) == start_hi[r : r + 1, :])
        b = onehot(iota((LANES, 128), 0) == start_lo[r : r + 1, :])
        marks = marks + dot(a, b, NT)
    marks = marks.astype(BF)
    incl = onehot(iota((LANES, LANES), 0) <= iota((LANES, LANES), 1))
    strict = onehot(iota((LANES, LANES), 0) < iota((LANES, LANES), 1))
    row_counts = dot(marks, jnp.ones((LANES, LANES), BF))
    below = onehot(iota((IDROWS, IDROWS), 1) < iota((IDROWS, IDROWS), 0))
    bag = (dot(marks, incl) + dot(below, row_counts.astype(BF))).astype(I32) - 1
    bag_ref[...] = bag
    key_ref[...] = owner_ref[...] * FEATS + (bag & (FEATS - 1))

    key_iota = iota((KEYS, LANES), 0)

    def count(r, acc):
        return acc + jnp.where(key_iota == key_ref[pl.ds(r, 1), :], 1.0, 0.0)

    counts = lax.fori_loop(0, IDROWS, count, jnp.zeros((KEYS, LANES), F32), unroll=4)
    totals = dot(counts.astype(BF), jnp.ones((LANES, LANES), BF))
    high = jnp.floor(totals * (1.0 / 256.0))
    low = totals - high * 256.0
    ki, kj = iota((KEYS, KEYS), 0), iota((KEYS, KEYS), 1)
    earlier = onehot((ki // FEATS == kj // FEATS) & (kj < ki))
    carry0 = dot(earlier, high.astype(BF)) * 256.0 + dot(earlier, low.astype(BF))

    rank_iota = iota((CAP // 2, LANES), 0)
    owner_iota = iota((OWNERS, LANES), 0)

    of_owner = onehot(iota((KEYS, OWNERS), 0) // FEATS == iota((KEYS, OWNERS), 1))
    by_owner = dot(of_owner, slot_ref[...].astype(F32).astype(BF), NT)
    is_feature = (iota((KEYS, FEATS), 0) & (FEATS - 1)) == iota((KEYS, FEATS), 1)
    slots = jnp.sum(jnp.where(is_feature, by_owner, 0.0), axis=1, keepdims=True)
    carry0 = carry0 + jnp.broadcast_to(slots, (KEYS, LANES)) * VOC

    def place(r, state):
        carry, acc = state
        same = key_iota == key_ref[pl.ds(r, 1), :]
        hot = jnp.where(same, 1.0, 0.0)
        prefix = dot(hot.astype(BF), strict)
        found = jnp.sum(jnp.where(same, prefix + carry, 0.0), axis=0, keepdims=True)
        found = found.astype(I32)
        rank = found & (VOC - 1)
        row = (found - rank) + ids_ref[pl.ds(r, 1), :]
        value = (1 << 23) + (row << 10) + bag_ref[pl.ds(r, 1), :]
        mine = owner_iota == owner_ref[pl.ds(r, 1), :]
        pieces = [
            jnp.where(mine, jnp.broadcast_to(p.astype(F32), (OWNERS, LANES)), 0.0)
            for p in (value & 255, (value >> 8) & 255, value >> 16)
        ]
        left = jnp.concatenate(pieces, axis=0).astype(BF)
        upper = rank >= CAP // 2
        left = jnp.concatenate([left * onehot(~upper), left * onehot(upper)], axis=0)
        right = onehot(rank_iota == (rank & (CAP // 2 - 1)))
        acc = acc + dot(left, right, NT)
        carry = carry + (prefix + hot)[:, LANES - 1 : LANES]
        return carry, acc

    _, acc = lax.fori_loop(
        0, IDROWS, place, (carry0, jnp.zeros((6 * OWNERS, CAP // 2), F32)), unroll=IDROWS
    )
    acc = jnp.concatenate([acc[: 3 * OWNERS], acc[3 * OWNERS :]], axis=1).astype(I32)
    packed = acc[:OWNERS] + (acc[OWNERS : 2 * OWNERS] << 8) + (acc[2 * OWNERS :] << 16)
    out_ref[...] = packed
    for c in range(CAP // 128):
        send_ref[:, c, :] = packed[:, c * 128 : (c + 1) * 128]


def index_call(ids, owners, lengths, slots):
    return pl.pallas_call(
        index_kernel,
        out_shape=[
            jax.ShapeDtypeStruct((OWNERS, CAP), I32),
            jax.ShapeDtypeStruct((OWNERS, CAP // 128, 128), I32),
        ],
        scratch_shapes=[
            pltpu.VMEM((IDROWS, LANES), I32),
            pltpu.VMEM((IDROWS, LANES), I32),
            pltpu.VMEM((BAGS // 128, 128), I32),
            pltpu.VMEM((IDROWS, LANES), I32),
            pltpu.VMEM((IDROWS, LANES), I32),
        ],
        compiler_params=pltpu.CompilerParams(vmem_limit_bytes=VMEM),
        name="index",
    )(ids, owners, lengths, slots)


def gather_kernel(offset, row_ref, table_ref, out_ref, wide, picked):
    step = pl.program_id(0)
    depth = out_ref.shape[1]

    @pl.when(step == 0)
    def _():
        wide[...] = table_ref[...].astype(F32)

    for part in range(LISTS):
        base = part * CAP + offset

        def some(i, _):
            at = i * 32
            rows = [wide[pl.ds(row_ref[base + at + j], 1), :] for j in range(32)]
            for j in range(32):
                picked[pl.ds(part * depth + at + j, 1), :] = rows[j]
            return 0

        lax.fori_loop(0, depth // 32, some, 0)
        out_ref[part] = picked[part * depth : (part + 1) * depth, :].astype(BF)


def gather_call(rows, table, offset, depth):
    return pl.pallas_call(
        functools.partial(gather_kernel, offset),
        out_shape=jax.ShapeDtypeStruct((OWNERS, depth, EMB), BF),
        grid=(OWNERS // LISTS,),
        in_specs=[
            pl.BlockSpec((LISTS * CAP,), lambda i: (i,), memory_space=pltpu.SMEM),
            pl.BlockSpec((ROWS, EMB), lambda i: (0, 0)),
        ],
        out_specs=pl.BlockSpec((LISTS, depth, EMB), lambda i: (i, 0, 0)),
        scratch_shapes=[pltpu.VMEM((ROWS, EMB), F32), pltpu.VMEM((LISTS * depth, EMB), F32)],
        compiler_params=pltpu.CompilerParams(vmem_limit_bytes=VMEM),
        name="gather",
    )(rows, table)


def sums_of(packed_ref, got_ref, step, at):
    rows, masked = [], []
    depth = got_ref.shape[1]
    group = packed_ref[pl.ds(pl.multiple_of(step * POOLED, POOLED), POOLED), at : at + depth]
    for i in range(POOLED):
        packed = group[i : i + 1, :]
        bag = packed & (BAGS - 1)
        sample = jnp.where(packed > 0, bag >> 3, -1)
        rows.append(onehot(iota((SAMPLES, depth), 0) == sample))
        feature = jnp.broadcast_to((bag & (FEATS - 1)).astype(F32), (EMB, depth)).T.astype(BF)
        own = got_ref[i]
        masked.append(
            jnp.concatenate(
                [jnp.where(feature == f, own, jnp.zeros((), BF)) for f in range(FEATS)], axis=1
            )
        )
    return dot(jnp.concatenate(rows, axis=1), jnp.concatenate(masked, axis=0))


def pool_kernel(at, got_ref, packed_ref, out_ref):
    step = pl.program_id(0)
    sums = sums_of(packed_ref, got_ref, step, at)

    @pl.when(step == 0)
    def _():
        out_ref[...] = sums

    @pl.when(step > 0)
    def _():
        out_ref[...] += sums


def pool_call(got, packed, at):
    depth = got.shape[1]
    return pl.pallas_call(
        functools.partial(pool_kernel, at),
        out_shape=jax.ShapeDtypeStruct((SAMPLES, WIDTH), F32),
        grid=(OWNERS // POOLED,),
        in_specs=[
            pl.BlockSpec((POOLED, depth, EMB), lambda i: (i, 0, 0)),
            pl.BlockSpec((OWNERS, CAP), lambda i: (0, 0)),
        ],
        out_specs=pl.BlockSpec((SAMPLES, WIDTH), lambda i: (0, 0)),
        compiler_params=pltpu.CompilerParams(vmem_limit_bytes=VMEM),
        name="pool",
    )(got, packed)


def sigmoid(x):
    return 1.0 / (1.0 + jnp.exp(-x))


def tower_kernel(
    at,
    me_ref,
    got_ref,
    packed_ref,
    earlier_ref,
    labels_ref,
    gain_ref,
    cbias_ref,
    dbias_ref,
    out_w_ref,
    cross_hbm,
    deep_hbm,
    logits_ref,
    kept_ref,
    given_ref,
    *refs,
):
    grad_refs = refs[:REPS]
    pooled_ref, cross_w, deep_w, start_ref, cross_t, deep_t, deep_s, gx_ref, sems, result_ref = refs[
        REPS:
    ]
    step = pl.program_id(0)

    def cross_copy(layer):
        return pltpu.make_async_copy(cross_hbm.at[layer], cross_w.at[layer], sems.at[layer])

    def deep_copy(layer):
        return pltpu.make_async_copy(deep_hbm.at[layer], deep_w.at[layer], sems.at[3 + layer])

    @pl.when(step == 0)
    def _():
        for layer in range(3):
            cross_copy(layer).start()
        for layer in range(3):
            deep_copy(layer).start()
        pooled_ref[...] = earlier_ref[...]

    pooled_ref[...] += sums_of(packed_ref, got_ref, step, at)

    @pl.when(step == OWNERS // POOLED - 1)
    def _():
        gain = gain_ref[...]
        pooled = pooled_ref[...]
        inverse = lax.rsqrt(jnp.mean(pooled * pooled, axis=1, keepdims=True) + 1e-06)
        start = (pooled * inverse * gain).astype(BF)
        start_ref[...] = start
        current = start
        for layer in range(3):
            cross_copy(layer).wait()
            product = dot(current, cross_w[layer]) + cbias_ref[layer : layer + 1, :]
            cross_t[layer] = product
            current = (start_ref[...].astype(F32) * product + current.astype(F32)).astype(BF)
        for layer in range(3):
            deep_copy(layer).wait()
            product = dot(current, deep_w[layer]) + dbias_ref[layer : layer + 1, :]
            deep_t[layer] = product
            sig = sigmoid(product)
            deep_s[layer] = sig
            current = (product * sig).astype(BF)
        out_w = out_w_ref[...]
        logits = jnp.sum(current.astype(F32) * out_w, axis=1, keepdims=True)
        logits_ref[...] = logits
        error = sigmoid(logits) - labels_ref[...].astype(F32)
        grad = error * out_w
        for layer in (2, 1, 0):
            product = deep_t[layer]
            sig = deep_s[layer]
            masked = (grad * sig * (1.0 + product * (1.0 - sig))).astype(BF)
            grad = dot(masked, deep_w[layer], NT)
        gx_ref[...] = jnp.zeros_like(gx_ref)
        for layer in (2, 1, 0):
            crossed = (grad * start_ref[...].astype(F32)).astype(BF)
            gx_ref[...] += grad * cross_t[layer]
            grad = grad + dot(crossed, cross_w[layer], NT)
            if layer == 0:
                outer = dot(start_ref[...], crossed, TN).reshape(CHIPS, CORES, REPS, 8, WIDTH)
                for core in range(CORES):

                    @pl.when(me_ref[1] == core)
                    def _():
                        for r in range(REPS):
                            kept_ref[r] = outer[:, core, r].reshape(CHIPS * 8, WIDTH).astype(BF)
                            given_ref[r] = (
                                outer[:, 1 - core, r].reshape(CHIPS * 8, WIDTH).astype(BF)
                            )
        scaled = (gx_ref[...] + grad) * gain
        pooled = pooled_ref[...]
        inverse = lax.rsqrt(jnp.mean(pooled * pooled, axis=1, keepdims=True) + 1e-06)
        mean = jnp.mean(scaled * pooled, axis=1, keepdims=True)
        result = (inverse * scaled - pooled * (inverse * inverse * inverse) * mean).astype(BF)
        result_ref[...] = result
        for k in range(REPS):
            block = (me_ref[0] + k) & (REPS - 1)
            columns = pl.ds(pl.multiple_of(block * (PAIR * EMB), PAIR * EMB), PAIR * EMB)
            grad_refs[k][...] = result_ref[:, columns]


def tower_call(me, got, packed, earlier, labels, gain, cross, cbias, deep, dbias, out_w):
    def whole(shape):
        return pl.BlockSpec(shape, lambda i: (0,) * len(shape))

    return pl.pallas_call(
        functools.partial(tower_kernel, CAP - got.shape[1]),
        grid=(OWNERS // POOLED,),
        in_specs=[
            pl.BlockSpec(memory_space=pltpu.SMEM),
            pl.BlockSpec((POOLED, got.shape[1], EMB), lambda i: (i, 0, 0)),
            whole((OWNERS, CAP)),
            whole((SAMPLES, WIDTH)),
            whole((SAMPLES, 1)),
            whole((1, WIDTH)),
            whole((3, WIDTH)),
            whole((3, WIDTH)),
            whole((1, WIDTH)),
            pl.BlockSpec(memory_space=pl.ANY),
            pl.BlockSpec(memory_space=pl.ANY),
        ],
        out_specs=[
            whole((SAMPLES, 1)),
            whole((REPS, CHIPS * 8, WIDTH)),
            whole((REPS, CHIPS * 8, WIDTH)),
        ]
        + [whole((SAMPLES, PAIR * EMB))] * REPS,
        out_shape=[
            jax.ShapeDtypeStruct((SAMPLES, 1), F32),
            jax.ShapeDtypeStruct((REPS, CHIPS * 8, WIDTH), BF),
            jax.ShapeDtypeStruct((REPS, CHIPS * 8, WIDTH), BF),
        ]
        + [jax.ShapeDtypeStruct((SAMPLES, PAIR * EMB), BF)] * REPS,
        scratch_shapes=[
            pltpu.VMEM((SAMPLES, WIDTH), F32),
            pltpu.VMEM((3, WIDTH, WIDTH), BF),
            pltpu.VMEM((3, WIDTH, WIDTH), BF),
            pltpu.VMEM((SAMPLES, WIDTH), BF),
            pltpu.VMEM((3, SAMPLES, WIDTH), F32),
            pltpu.VMEM((3, SAMPLES, WIDTH), F32),
            pltpu.VMEM((3, SAMPLES, WIDTH), F32),
            pltpu.VMEM((SAMPLES, WIDTH), F32),
            pltpu.SemaphoreType.DMA((6,)),
            pltpu.VMEM((SAMPLES, WIDTH), BF),
        ],
        compiler_params=pltpu.CompilerParams(vmem_limit_bytes=VMEM),
        name="tower",
    )(me, got, packed, earlier, labels, gain, cbias, dbias, out_w, cross, deep)


def scatter_kernel(first_ref, trips_ref, word_ref, grads_ref, out_ref, wide, *accs):
    step = pl.program_id(0)

    @pl.when(step == 0)
    def _():
        for acc in accs:
            acc[...] = jnp.zeros_like(acc)

    group = grads_ref.shape[0]
    for g in range(group):
        for r in range(REPS):
            block = grads_ref[g, r]
            base = (g * REPS + r) * PAIR * SAMPLES
            for f in range(PAIR):
                wide[base + f * SAMPLES : base + (f + 1) * SAMPLES, :] = block[
                    :, f * EMB : (f + 1) * EMB
                ].astype(F32)

    def device(k, _):
        listed = step * group * REPS + k
        first = first_ref[listed]

        def some(i, _):
            at = first + i * ACCS
            words = [word_ref[at + j] for j in range(ACCS)]
            rows = [wide[pl.ds(word & (SOURCES - 1), 1), :] for word in words]
            olds = [accs[j][pl.ds(words[j] >> SHIFT, 1), :] for j in range(ACCS)]
            for j in range(ACCS):
                accs[j][pl.ds(words[j] >> SHIFT, 1), :] = olds[j] + rows[j]
            return 0

        lax.fori_loop(0, trips_ref[listed], some, 0)
        return 0

    lax.fori_loop(0, group * REPS, device, 0)

    @pl.when(step == pl.num_programs(0) - 1)
    def _():
        total = accs[0][: PAIR * VOC, :]
        for acc in accs[1:]:
            total = total + acc[: PAIR * VOC, :]
        out_ref[...] = total.astype(out_ref.dtype)


def scatter_call(words, first, trips, grads, group=GROUP):
    rows = PAIR * VOC
    return pl.pallas_call(
        scatter_kernel,
        out_shape=jax.ShapeDtypeStruct((rows, EMB), BF),
        grid_spec=pltpu.PrefetchScalarGridSpec(
            num_scalar_prefetch=2,
            grid=(OWNERS // group,),
            in_specs=[
                pl.BlockSpec(
                    (group * REPS * LISTED,), lambda i, *_: (i,), memory_space=pltpu.SMEM
                ),
                pl.BlockSpec(
                    (group, REPS, SAMPLES, PAIR * EMB), lambda i, *_: (i, 0, 0, 0)
                ),
            ],
            out_specs=pl.BlockSpec((rows, EMB), lambda i, *_: (0, 0)),
            scratch_shapes=[pltpu.VMEM((group * REPS * PAIR * SAMPLES, EMB), F32)]
            + [pltpu.VMEM((rows + 8, EMB), F32) for _ in range(ACCS)],
        ),
        compiler_params=pltpu.CompilerParams(vmem_limit_bytes=VMEM),
        name="scatter",
    )(first, trips, words, grads)


def finish_kernel(count, place_ref, *refs):
    blocks, (out, wide, sems) = refs[:count], refs[-3:]
    copies = []
    n = 0
    for block in blocks:
        for f in range(block.shape[0]):
            wide[n] = block[f].astype(F32)
            to = pl.multiple_of(place_ref[n] * VOC, VOC)
            copies.append(
                pltpu.make_async_copy(wide.at[n], out.at[pl.ds(to, VOC), :], sems.at[n])
            )
            copies[-1].start()
            n += 1
    for copy in copies:
        copy.wait()


def finish_call(places, blocks, earlier=None):
    more = [] if earlier is None else [earlier]
    total = sum(block.shape[0] for block in blocks)
    return pl.pallas_call(
        functools.partial(finish_kernel, len(blocks)),
        out_shape=jax.ShapeDtypeStruct((ROWS, EMB), F32),
        in_specs=[pl.BlockSpec(memory_space=pltpu.SMEM)]
        + [pl.BlockSpec(memory_space=pltpu.VMEM) for _ in blocks]
        + [pl.BlockSpec(memory_space=pl.ANY) for _ in more],
        out_specs=pl.BlockSpec(memory_space=pl.ANY),
        scratch_shapes=[
            pltpu.VMEM((total, VOC, EMB), F32),
            pltpu.SemaphoreType.DMA((total,)),
        ],
        input_output_aliases={1 + len(blocks): 0} if more else {},
        compiler_params=pltpu.CompilerParams(vmem_limit_bytes=16 * 1024 * 1024),
        name="finish",
    )(places, *blocks, *more)


def from_before(x, axis, k):
    if k == 0:
        return x
    n = lax.axis_size(axis)
    return lax.ppermute(x, axis, [(i, (i + k) % n) for i in range(n)])


def in_order(x, axis, me):
    n = lax.axis_size(axis)
    back = [from_before(x, axis, k) for k in range(n)]
    twice = jnp.concatenate([back[(n - 1 - i) % n] for i in range(2 * n - 1)])
    return lax.dynamic_slice_in_dim(twice, (n - 1 - me) * x.shape[0], n * x.shape[0])


def summed(x):
    return jnp.sum(x.astype(F32), axis=0).astype(BF)


def body(
    embed_table,
    row_ids,
    row_owner,
    lengths,
    feature_slot,
    labels,
    norm_gain,
    cross_weight,
    cross_bias,
    deep_weight,
    deep_bias,
    out_weight,
):
    packed, sent = index_call(
        row_ids,
        row_owner.reshape(1, IDS),
        lengths,
        feature_slot.T,
    )
    asked = lax.all_to_all(sent, "shard", split_axis=0, concat_axis=0, tiled=True)
    rows = ((asked >> 10) & (ROWS - 1)).reshape(-1)

    def exchange(x, axis):
        return lax.all_to_all(x, axis, split_axis=0, concat_axis=0, tiled=True)

    picked_early = gather_call(rows, embed_table, 0, EARLY)
    picked_early, lists = lax.optimization_barrier((picked_early, asked))
    got_early = exchange(picked_early, "shard")
    picked_late, lists = lax.optimization_barrier(
        (gather_call(rows, embed_table, EARLY, CAP - EARLY), lists)
    )
    got_late = exchange(picked_late, "shard")

    rep = lax.axis_index("rep")
    everyone = jnp.stack(
        [
            from_before(lists, "rep", k).reshape(OWNERS // GROUP, GROUP, CAP)
            for k in range(REPS)
        ],
        axis=2,
    )
    feature = everyone & (FEATS - 1)
    valid = everyone > 0
    within = feature - rep * PAIR
    ours = valid & (within >= 0) & (within < PAIR)
    target = jnp.where(ours, within * VOC + ((everyone >> 10) & (VOC - 1)), PAIR * VOC)
    group = lax.broadcasted_iota(I32, everyone.shape, 1)
    back = lax.broadcasted_iota(I32, everyone.shape, 2)
    source = (group * REPS + back) * (PAIR * SAMPLES) + jnp.where(
        ours, within * SAMPLES + ((everyone >> 3) & (SAMPLES - 1)), 0
    )
    words = jnp.pad(
        (target << SHIFT) | source,
        ((0, 0), (0, 0), (0, 0), (0, LISTED - CAP)),
        constant_values=(PAIR * VOC) << SHIFT,
    ).reshape(-1)
    below = jnp.sum((valid & (within < 0)).astype(I32), axis=3)
    upto = jnp.sum((valid & (within < PAIR)).astype(I32), axis=3)
    places = lax.broadcasted_iota(I32, below.shape, 1) * REPS + lax.broadcasted_iota(
        I32, below.shape, 2
    )
    first_word = (places * LISTED + below).reshape(-1)
    trips = ((upto - below + ACCS - 1) >> (ACCS.bit_length() - 1)).reshape(-1)
    sums_early = pool_call(got_early, packed, 0)
    slots = feature_slot[lax.axis_index("shard")]
    holder = (rep - jnp.array([0, 1, 3, 2], I32)) % REPS
    features = holder[:, None] * PAIR + jnp.arange(PAIR, dtype=I32)[None, :]
    places = slots[features.reshape(-1)]
    got_late, sums_early, words, first_word, trips, places = lax.optimization_barrier(
        (got_late, sums_early, words, first_word, trips, places)
    )

    logits, kept, given, *grads = tower_call(
        jnp.stack([rep, lax.axis_index("shard") % CORES]).astype(I32),
        got_late,
        packed,
        sums_early,
        labels.reshape(SAMPLES, 1),
        norm_gain.reshape(1, WIDTH),
        cross_weight,
        cross_bias,
        deep_weight,
        deep_bias,
        out_weight.reshape(1, WIDTH),
    )
    mine = jnp.stack([from_before(grads[k], "rep", k) for k in range(REPS)])
    mine, kept, given = lax.optimization_barrier((mine, kept, given))
    all_grads = lax.all_gather(mine, "shard", axis=0)
    other = lax.ppermute(given, "shard", [(i, i ^ 1) for i in range(OWNERS)])
    half = (kept.astype(F32) + other.astype(F32)).astype(BF)
    quarter = summed(exchange(half, "rep"))
    eight = summed(
        lax.all_to_all(
            quarter.reshape(CHIPS, 8, WIDTH),
            "shard",
            split_axis=0,
            concat_axis=0,
            axis_index_groups=[list(range(c, OWNERS, CORES)) for c in range(CORES)],
            tiled=True,
        )
    )
    first_grad = lax.all_gather(
        in_order(eight, "rep", rep), "shard", axis=0, tiled=True
    ).astype(F32)

    part = scatter_call(words, first_word, trips, all_grads).reshape(PAIR, VOC, EMB)
    before = from_before(part, "rep", 1)
    after = from_before(part, "rep", REPS - 1)
    across = [
        from_before(before[:1], "rep", 1),
        from_before(after[1:], "rep", REPS - 1),
    ]
    near, far = places[: 3 * PAIR], places[3 * PAIR :]
    row_grad = finish_call(near, [part, before, after])
    row_grad = finish_call(far, across, row_grad)
    return (row_grad, first_grad, logits.reshape(SAMPLES))


def solution(mesh):
    both = ("rep", "shard")
    in_specs = (
        P("shard", None),
        P(both, None),
        P(both, None, None),
        P(both, None),
        P(),
        P(both),
        P(),
        P(),
        P(),
        P(),
        P(),
        P(),
    )
    out_specs = (P("shard", None), P(), P(both))
    return jax.shard_map(body, mesh=mesh, in_specs=in_specs, out_specs=out_specs, check_vma=False)
```

profile of v0, /device:TPU:70, one launch (start us, length us, event | category | flops | bytes accessed | tf_op | source)
XLA Modules:
  0.0 256.3 jit_solution(1269034650125288095)
XLA Ops:
  7.2 9.1 %index.1 = (s32[32,512]{1,0:T(8,128)}, s32[32,4,128]{2,1,0:T(4,128)}) custom-call(s32[1,8192]{1,0:T(1,128)} %ids_in.1, s32[1,8192]{1,0:T(1,128)} %bitcast.38, s32[1,1024]{1,0:T(1,128)} %len_in.1, s32[8,32]{1,0:T(8,128)} %bitcast.39), custom_call_target="tpu_custom_call" | custom-call | tf_op jit(solution)/shard_map/index/pallas_call | solution.py:146
  16.3 11.3 %all_to_all.25 = s32[32,4,128]{2,1,0:T(4,128)S(1)} all-to-all(s32[32,4,128]{2,1,0:T(4,128)} %get-tuple-element.25), channel_id=1, replica_groups=mesh['rep'=4,'shard'=32] {'shard'}, dimensions={0} | all-to-all | bytes 131072 | tf_op jit(solution)/shard_map/all_to_all | solution.py:545
  28.2 6.6 %gather.9 = bf16[32,128,128]{2,1,0:T(8,128)(2,1)} custom-call(s32[16384]{0:T(1024)} %bitcast.29, bf16[8192,128]{1,0:T(8,128)(2,1)} %table_ref.3), custom_call_target="tpu_custom_call" | custom-call | tf_op jit(solution)/shard_map/gather/pallas_call | solution.py:187
  34.9 7.7 %all-to-all-start.2 = ((bf16[32,128,128]{2,1,0:T(8,128)(2,1)}), bf16[32,128,128]{2,1,0:T(8,128)(2,1)S(1)}, u32[]{:S(2)}, u32[]{:S(2)}) async-start(bf16[32,128,128]{2,1,0:T(8,128)(2,1)} %gather.9), calls=%async_computation.2 | async-start | bytes 2097152 | tf_op jit(solution)/shard_map/all_to_all | solution.py:549
  42.6 14.8 %gather.8 = bf16[32,384,128]{2,1,0:T(8,128)(2,1)} custom-call(s32[16384]{0:T(1024)} %bitcast.30, bf16[8192,128]{1,0:T(8,128)(2,1)} %table_ref.3), custom_call_target="tpu_custom_call" | custom-call | tf_op jit(solution)/shard_map/gather/pallas_call | solution.py:187
  58.4 7.4 %all-to-all-start.1 = ((bf16[32,384,128]{2,1,0:T(8,128)(2,1)}), bf16[32,384,128]{2,1,0:T(8,128)(2,1)}, u32[]{:S(2)}, u32[]{:S(2)}) async-start(bf16[32,384,128]{2,1,0:T(8,128)(2,1)} %gather.8), calls=%async_computation.1 | async-start | bytes 6291456 | tf_op jit(solution)/shard_map/all_to_all | solution.py:549
  67.6 3.1 %collective-permute-start.2 = (s32[32,4,128]{2,1,0:T(4,128)S(1)}, s32[32,4,128]{2,1,0:T(4,128)S(1)}, u32[]{:S(2)}, u32[]{:S(2)}) collective-permute-start(s32[32,4,128]{2,1,0:T(4,128)S(1)} %all_to_all.25), channel_id=1, source_target_pairs={{0,96},{32,0},{64,32},{96,64},{1,97},{33,1},{65,33},{97,65},{2,98}... | collective-permute-start | bytes 196616 | tf_op jit(solution)/shard_map/ppermute | solution.py:511
  73.9 3.0 %collective-permute-done.1 = s32[32,4,128]{2,1,0:T(4,128)S(1)} collective-permute-done((s32[32,4,128]{2,1,0:T(4,128)S(1)}, s32[32,4,128]{2,1,0:T(4,128)S(1)}, u32[]{:S(2)}, u32[]{:S(2)}) %collective-permute-start.1) | collective-permute-done | bytes 65568 | tf_op jit(solution)/shard_map/ppermute | solution.py:511
  81.4 3.6 %pool.1.earlier_ref = f32[128,1024]{1,0:T(8,128)} custom-call(bf16[32,128,128]{2,1,0:T(8,128)(2,1)} %copy-done.1, s32[32,512]{1,0:T(8,128)} %get-tuple-element.29.packed_ref), custom_call_target="tpu_custom_call" | custom-call | tf_op jit(solution)/shard_map/pool/pallas_call | solution.py:236
  85.0 18.5 %all-to-all-done.1.got_ref = bf16[32,384,128]{2,1,0:T(8,128)(2,1)} async-done(((bf16[32,384,128]{2,1,0:T(8,128)(2,1)}), bf16[32,384,128]{2,1,0:T(8,128)(2,1)}, u32[]{:S(2)}, u32[]{:S(2)}) %all-to-all-start.1) | async-done | bytes 3145760 | tf_op jit(solution)/shard_map/all_to_all | solution.py:549
  103.5 15.4 %tower.1 = (f32[128,1]{1,0:T(8,128)}, bf16[4,128,1024]{2,1,0:T(8,128)(2,1)}, bf16[4,128,1024]{2,1,0:T(8,128)(2,1)}, bf16[128,256]{1,0:T(8,128)(2,1)}, bf16[128,2...) custom-call(s32[2]{0:T(128)} %pad_add_fusion.1.me_ref, ...), custom_call_target="tpu_custom_call" | custom-call | tf_op jit(solution)/shard_map/tower/pallas_call | solution.py:356
  118.9 3.1 %collective-permute-start.5 = (bf16[128,256]{1,0:T(8,128)(2,1)}, bf16[128,256]{1,0:T(8,128)(2,1)S(1)}, u32[]{:S(2)}, u32[]{:S(2)}) collective-permute-start(bf16[128,256]{1,0:T(8,128)(2,1)} %get-tuple-element.40), channel_id=1, source_target_pairs={{0,96},{32,0},{64,32},{96,64},{1,97},{33,1},{65,33},{97,65},{2,98}... | collective-permute-start | bytes 196616 | tf_op jit(solution)/shard_map/ppermute | solution.py:511
  124.3 3.8 %collective-permute-done.4 = bf16[128,256]{1,0:T(8,128)(2,1)S(1)} collective-permute-done((bf16[128,256]{1,0:T(8,128)(2,1)}, bf16[128,256]{1,0:T(8,128)(2,1)S(1)}, u32[]{:S(2)}, u32[]{:S(2)}) %collective-permute-start.4) | collective-permute-done | bytes 65568 | tf_op jit(solution)/shard_map/ppermute | solution.py:511
  130.5 2.9 %collective-permute-done.10 = bf16[4,128,1024]{2,1,0:T(8,128)(2,1)S(1)} collective-permute-done((bf16[4,128,1024]{2,1,0:T(8,128)(2,1)}, bf16[4,128,1024]{2,1,0:T(8,128)(2,1)S(1)}, u32[]{:S(2)}, u32[]{:S(2)}) %collective-permute-start.10) | collective-permute-done | bytes 1048608 | tf_op jit(solution)/shard_map/ppermute | solution.py:614
  134.9 18.1 %all_to_all.26 = bf16[4,128,1024]{2,1,0:T(8,128)(2,1)S(1)} all-to-all(bf16[4,128,1024]{2,1,0:T(8,128)(2,1)S(1)} %add_convert_fusion), channel_id=1, replica_groups=mesh['rep'=4,'shard'=32] {'rep'}, dimensions={0} | all-to-all | bytes 2097152 | tf_op jit(solution)/shard_map/all_to_all | solution.py:549
  153.2 13.6 %all_to_all.27 = bf16[16,8,1024]{2,1,0:T(8,128)(2,1)S(1)} all-to-all(bf16[16,8,1024]{2,1,0:T(8,128)(2,1)S(1)} %bitcast.27), channel_id=1, replica_groups={{0,2,4,6,8,10,12,14,16,18,20,22,24,26,28,30},{1,3,5,7,9,11,13,15,17,19,..., dimensions={0} | all-to-all | bytes 524288 | tf_op jit(solution)/shard_map/all_to_all | solution.py:618
  166.9 1.8 collective-permute-start.12
  174.3 8.4 %all-gather.6.cloned.1.call-done = bf16[128,128,256]{2,1,0:T(8,128)(2,1)} async-done(((bf16[4,128,256]{2,1,0:T(8,128)(2,1)}), bf16[128,128,256]{2,1,0:T(8,128)(2,1)}) %all-gather.6.cloned.1.call-update) | async-done | bytes 8388624 | tf_op jit(solution)/shard_map/all_gather | solution.py:613
  182.8 43.9 %scatter.1 = bf16[2048,128]{1,0:T(8,128)(2,1)} custom-call(s32[128]{0:T(128)} %add.93.first_ref, s32[128]{0:T(128)} %reshape.89.trips_ref, s32[73728]{0:T(1024)} %reshape.81.word_ref, bf16[32,4,128,256]{3,2,1,0:T(8,128)(2,1)} %bitcast.26), custom_call_target="tpu_custom_call" | custom-call | tf_op jit(solution)/shard_map/scatter/pallas_call | solution.py:447
  227.2 2.7 %collective-permute-start.8 = (bf16[2,1024,128]{2,1,0:T(8,128)(2,1)}, bf16[2,1024,128]{2,1,0:T(8,128)(2,1)S(1)}, u32[]{:S(2)}, u32[]{:S(2)}) collective-permute-start(bf16[2,1024,128]{2,1,0:T(8,128)(2,1)} %bitcast.23), channel_id=1, source_target_pairs={{0,96},{32,0},{64,32},{96,64},{1,97},{33,1},{65,33},{97,65},{2,98}... | collective-permute-start | bytes 1572872 | tf_op jit(solution)/shard_map/ppermute | solution.py:511
  229.9 7.4 %collective-permute-done.6.refs_1_ = bf16[2,1024,128]{2,1,0:T(8,128)(2,1)S(1)} collective-permute-done((bf16[2,1024,128]{2,1,0:T(8,128)(2,1)}, bf16[2,1024,128]{2,1,0:T(8,128)(2,1)S(1)}, u32[]{:S(2)}, u32[]{:S(2)}) %collective-permute-start.6) | collective-permute-done | bytes 524320 | tf_op jit(solution)/shard_map/ppermute | solution.py:511
  237.4 3.3 %collective-permute-start.9 = (bf16[1,1024,128]{2,1,0:T(8,128)(2,1)S(1)}, bf16[1,1024,128]{2,1,0:T(8,128)(2,1)S(1)}, u32[]{:S(2)}, u32[]{:S(2)}) collective-permute-start(bf16[1,1024,128]{2,1,0:T(8,128)(2,1)S(1)} %slice.19), channel_id=1, source_target_pairs={{0,96},{32,0},{64,32},{96,64},{1,97},{33,1},{65,33},{97,65},{2,98}... | collective-permute-start | bytes 786440 | tf_op jit(solution)/shard_map/ppermute | solution.py:511
  241.4 4.1 %convert_element_type.27 = f32[1024,1024]{1,0:T(8,128)} convert(bf16[1024,1024]{1,0:T(8,128)(2,1)} %all-gather.4.cloned.1.call-done) | non-fusion elementwise | flops 1048576 | bytes 6291456 | tf_op jit(solution)/shard_map/convert_element_type | solution.py:629
  245.5 2.3 finish.2.refs_2_
  (71 shorter events, 26.2 us)
Async XLA Ops:
  34.9 22.5 %all-to-all-start.2 = ((bf16[32,128,128]{2,1,0:T(8,128)(2,1)}), bf16[32,128,128]{2,1,0:T(8,128)(2,1)S(1)}, u32[]{:S(2)}, u32[]{:S(2)}) async-start(bf16[32,128,128]{2,1,0:T(8,128)(2,1)} %gather.9), calls=%async_computation.2 | async-start | bytes 2097152 | tf_op jit(solution)/shard_map/all_to_all | solution.py:549
  57.4 8.5 %copy-start.3 = (s32[32,8]{0,1:T(8,128)S(1)}, s32[32,8]{0,1:T(8,128)}, u32[]{:S(2)}) copy-start(s32[32,8]{0,1:T(8,128)} %param.17) | copy-start | bytes 3076
  57.4 8.7 %copy-start.5 = (s32[4]{0:T(128)S(1)}, s32[4]{0:T(128)}, u32[]{:S(2)}) copy-start(s32[4]{0:T(128)} %constant.94) | copy-start | bytes 52
  57.4 8.9 %copy-start.4 = (s32[128]{0:T(128)S(1)}, s32[128]{0:T(128)}, u32[]{:S(2)}) copy-start(s32[128]{0:T(128)} %param.18) | copy-start | bytes 1540
  57.4 1.0 copy-start.1
  58.4 45.1 %all-to-all-start.1 = ((bf16[32,384,128]{2,1,0:T(8,128)(2,1)}), bf16[32,384,128]{2,1,0:T(8,128)(2,1)}, u32[]{:S(2)}, u32[]{:S(2)}) async-start(bf16[32,384,128]{2,1,0:T(8,128)(2,1)} %gather.8), calls=%async_computation.1 | async-start | bytes 6291456 | tf_op jit(solution)/shard_map/all_to_all | solution.py:549
  65.8 117.0 %all-gather.6.cloned.1.call-start = ((), (), s32[]{:S(2)}) async-start(), calls=%async_computation.6 | async-start | bytes 8650752 | tf_op jit(solution)/shard_map/all_gather | solution.py:613
  67.6 6.2 %collective-permute-start.2 = (s32[32,4,128]{2,1,0:T(4,128)S(1)}, s32[32,4,128]{2,1,0:T(4,128)S(1)}, u32[]{:S(2)}, u32[]{:S(2)}) collective-permute-start(s32[32,4,128]{2,1,0:T(4,128)S(1)} %all_to_all.25), channel_id=1, source_target_pairs={{0,96},{32,0},{64,32},{96,64},{1,97},{33,1},{65,33},{97,65},{2,98}... | collective-permute-start | bytes 196616 | tf_op jit(solution)/shard_map/ppermute | solution.py:511
  70.7 6.1 %collective-permute-start.1 = (s32[32,4,128]{2,1,0:T(4,128)S(1)}, s32[32,4,128]{2,1,0:T(4,128)S(1)}, u32[]{:S(2)}, u32[]{:S(2)}) collective-permute-start(s32[32,4,128]{2,1,0:T(4,128)S(1)} %all_to_all.25), channel_id=1, source_target_pairs={{0,64},{32,96},{64,0},{96,32},{1,65},{33,97},{65,1},{97,33},{2,66}... | collective-permute-start | bytes 196616 | tf_op jit(solution)/shard_map/ppermute | solution.py:511
  71.4 6.1 %collective-permute-start = (s32[32,4,128]{2,1,0:T(4,128)S(1)}, s32[32,4,128]{2,1,0:T(4,128)S(1)}, u32[]{:S(2)}, u32[]{:S(2)}) collective-permute-start(s32[32,4,128]{2,1,0:T(4,128)S(1)} %all_to_all.25), channel_id=1, source_target_pairs={{0,32},{32,64},{64,96},{96,0},{1,33},{33,65},{65,97},{97,1},{2,34}... | collective-permute-start | bytes 196616 | tf_op jit(solution)/shard_map/ppermute | solution.py:511
  118.9 5.4 %collective-permute-start.5 = (bf16[128,256]{1,0:T(8,128)(2,1)}, bf16[128,256]{1,0:T(8,128)(2,1)S(1)}, u32[]{:S(2)}, u32[]{:S(2)}) collective-permute-start(bf16[128,256]{1,0:T(8,128)(2,1)} %get-tuple-element.40), channel_id=1, source_target_pairs={{0,96},{32,0},{64,32},{96,64},{1,97},{33,1},{65,33},{97,65},{2,98}... | collective-permute-start | bytes 196616 | tf_op jit(solution)/shard_map/ppermute | solution.py:511
  122.0 6.0 %collective-permute-start.4 = (bf16[128,256]{1,0:T(8,128)(2,1)}, bf16[128,256]{1,0:T(8,128)(2,1)S(1)}, u32[]{:S(2)}, u32[]{:S(2)}) collective-permute-start(bf16[128,256]{1,0:T(8,128)(2,1)} %get-tuple-element.39), channel_id=1, source_target_pairs={{0,64},{32,96},{64,0},{96,32},{1,65},{33,97},{65,1},{97,33},{2,66}... | collective-permute-start | bytes 196616 | tf_op jit(solution)/shard_map/ppermute | solution.py:511
  122.6 6.1 %collective-permute-start.3 = (bf16[128,256]{1,0:T(8,128)(2,1)}, bf16[128,256]{1,0:T(8,128)(2,1)S(1)}, u32[]{:S(2)}, u32[]{:S(2)}) collective-permute-start(bf16[128,256]{1,0:T(8,128)(2,1)} %get-tuple-element.38), channel_id=1, source_target_pairs={{0,32},{32,64},{64,96},{96,0},{1,33},{33,65},{65,97},{97,1},{2,34}... | collective-permute-start | bytes 196616 | tf_op jit(solution)/shard_map/ppermute | solution.py:511
  130.3 111.1 %all-gather.4.cloned.1.call-start = ((), (), s32[]{:S(2)}) async-start(), calls=%async_computation.5 | async-start | bytes 2162688 | tf_op jit(solution)/shard_map/all_gather | solution.py:627
  130.4 3.0 %collective-permute-start.10 = (bf16[4,128,1024]{2,1,0:T(8,128)(2,1)}, bf16[4,128,1024]{2,1,0:T(8,128)(2,1)S(1)}, u32[]{:S(2)}, u32[]{:S(2)}) collective-permute-start(bf16[4,128,1024]{2,1,0:T(8,128)(2,1)} %get-tuple-element.45), channel_id=1, source_target_pairs={{0,1},{1,0},{2,3},{3,2},{4,5},{5,4},{6,7},{7,6},{8,9},{9,8},{10,11... | collective-permute-start | bytes 3145736 | tf_op jit(solution)/shard_map/ppermute | solution.py:614
  166.8 3.8 %collective-permute-start.11 = (bf16[8,1024]{1,0:T(8,128)(2,1)S(1)}, bf16[8,1024]{1,0:T(8,128)(2,1)S(1)}, u32[]{:S(2)}, u32[]{:S(2)}) collective-permute-start(bf16[8,1024]{1,0:T(8,128)(2,1)S(1)} %reduce_sum.45), channel_id=1, source_target_pairs={{0,96},{32,0},{64,32},{96,64},{1,97},{33,1},{65,33},{97,65},{2,98}... | collective-permute-start | bytes 49160 | tf_op jit(solution)/shard_map/ppermute | solution.py:511
  166.9 5.3 %collective-permute-start.12 = (bf16[8,1024]{1,0:T(8,128)(2,1)S(1)}, bf16[8,1024]{1,0:T(8,128)(2,1)S(1)}, u32[]{:S(2)}, u32[]{:S(2)}) collective-permute-start(bf16[8,1024]{1,0:T(8,128)(2,1)S(1)} %reduce_sum.45), channel_id=1, source_target_pairs={{0,64},{32,96},{64,0},{96,32},{1,65},{33,97},{65,1},{97,33},{2,66}... | collective-permute-start | bytes 49160 | tf_op jit(solution)/shard_map/ppermute | solution.py:511
  168.7 4.9 %collective-permute-start.13 = (bf16[8,1024]{1,0:T(8,128)(2,1)S(1)}, bf16[8,1024]{1,0:T(8,128)(2,1)S(1)}, u32[]{:S(2)}, u32[]{:S(2)}) collective-permute-start(bf16[8,1024]{1,0:T(8,128)(2,1)S(1)} %reduce_sum.45), channel_id=1, source_target_pairs={{0,32},{32,64},{64,96},{96,0},{1,33},{33,65},{65,97},{97,1},{2,34}... | collective-permute-start | bytes 49160 | tf_op jit(solution)/shard_map/ppermute | solution.py:511
  182.8 58.0 %copy-start.2 = (f32[128,1]{1,0:T(8,128)S(1)}, f32[128,1]{1,0:T(8,128)}, u32[]{:S(2)}) copy-start(f32[128,1]{1,0:T(8,128)} %get-tuple-element.46) | copy-start | bytes 1540
  226.7 10.6 %collective-permute-start.6 = (bf16[2,1024,128]{2,1,0:T(8,128)(2,1)}, bf16[2,1024,128]{2,1,0:T(8,128)(2,1)S(1)}, u32[]{:S(2)}, u32[]{:S(2)}) collective-permute-start(bf16[2,1024,128]{2,1,0:T(8,128)(2,1)} %bitcast.22), channel_id=1, source_target_pairs={{0,32},{32,64},{64,96},{96,0},{1,33},{33,65},{65,97},{97,1},{2,34}... | collective-permute-start | bytes 1572872 | tf_op jit(solution)/shard_map/ppermute | solution.py:511
  227.2 10.2 %collective-permute-start.8 = (bf16[2,1024,128]{2,1,0:T(8,128)(2,1)}, bf16[2,1024,128]{2,1,0:T(8,128)(2,1)S(1)}, u32[]{:S(2)}, u32[]{:S(2)}) collective-permute-start(bf16[2,1024,128]{2,1,0:T(8,128)(2,1)} %bitcast.23), channel_id=1, source_target_pairs={{0,96},{32,0},{64,32},{96,64},{1,97},{33,1},{65,33},{97,65},{2,98}... | collective-permute-start | bytes 1572872 | tf_op jit(solution)/shard_map/ppermute | solution.py:511
  237.3 10.5 %collective-permute-start.7 = (bf16[1,1024,128]{2,1,0:T(8,128)(2,1)S(1)}, bf16[1,1024,128]{2,1,0:T(8,128)(2,1)S(1)}, u32[]{:S(2)}, u32[]{:S(2)}) collective-permute-start(bf16[1,1024,128]{2,1,0:T(8,128)(2,1)S(1)} %slice.18), channel_id=1, source_target_pairs={{0,32},{32,64},{64,96},{96,0},{1,33},{33,65},{65,97},{97,1},{2,34}... | collective-permute-start | bytes 786440 | tf_op jit(solution)/shard_map/ppermute | solution.py:511
  237.4 10.4 %collective-permute-start.9 = (bf16[1,1024,128]{2,1,0:T(8,128)(2,1)S(1)}, bf16[1,1024,128]{2,1,0:T(8,128)(2,1)S(1)}, u32[]{:S(2)}, u32[]{:S(2)}) collective-permute-start(bf16[1,1024,128]{2,1,0:T(8,128)(2,1)S(1)} %slice.19), channel_id=1, source_target_pairs={{0,96},{32,0},{64,32},{96,64},{1,97},{33,1},{65,33},{97,65},{2,98}... | collective-permute-start | bytes 786440 | tf_op jit(solution)/shard_map/ppermute | solution.py:511
  241.4 4.1 %copy-start = (bf16[2048,128]{1,0:T(8,128)(2,1)S(1)}, bf16[2048,128]{1,0:T(8,128)(2,1)}, u32[]{:S(2)}) copy-start(bf16[2048,128]{1,0:T(8,128)(2,1)} %scatter.1) | copy-start | bytes 1572868
Sparse Core Ops, SparseCore 0:
  130.4 52.2 all-gather.5
  185.6 41.7 all-gather.3
where the time goes:
time: 258 us; the launch traced here: 256 us
  Pallas kernels  97.3 us (38%)
  waiting for transfers between devices  51.5 us (20%)
  blocking collectives  43 us (17%)
  starting transfers between devices  33.4 us (13%)
  between operations  14.3 us (6%)
  other arithmetic  11 us (4%)
  local copies, waits for them, and re-layouts  5.84 us (2%)
    pallas_call x1, Pallas kernels, scatter_call(): pl.pallas_call(scatter_kernel, out_shape=jax.ShapeDtypeStruct((rows, EMB)...  43.9 us
    ppermute x13, waiting for transfers between devices, from_before(): return lax.ppermute(x, axis, [(i, (i + k) % n) for i in range(n)])  21.8 us
    pallas_call x2, Pallas kernels, gather_call(): pl.pallas_call(functools.partial(gather_kernel, offset), out_shape=jax.Sh...  21.4 us
    all_to_all x2, waiting for transfers between devices, exchange(): return lax.all_to_all(x, axis, split_axis=0, concat_axis=0, tiled=True)  18.5 us
    all_to_all x1, blocking collectives, exchange(): return lax.all_to_all(x, axis, split_axis=0, concat_axis=0, tiled=True)  18.1 us
    ppermute x13, starting transfers between devices, from_before(): return lax.ppermute(x, axis, [(i, (i + k) % n) for i in range(n)])  18.1 us
    pallas_call x1, Pallas kernels, tower_call(): pl.pallas_call(functools.partial(tower_kernel, CAP - got.shape[1]), grid=...  15.4 us
    all_to_all x2, starting transfers between devices, exchange(): return lax.all_to_all(x, axis, split_axis=0, concat_axis=0, tiled=True)  15.2 us
  transfers between devices with their start and end apart: 18, of which 13 were waited for; matrix products, arithmetic and copies ran while one was open for 5% of the time, Pallas kernels for 25%

commit v1 on v0

--- a/solution.py
+++ b/solution.py
@@ -504,6 +504,29 @@
     )(places, *blocks, *more)
 
 
+def join_kernel(*refs):
+    blocks, (out, sems) = refs[:-2], refs[-2:]
+    copies = [
+        pltpu.make_async_copy(block, out.at[k], sems.at[k]) for k, block in enumerate(blocks)
+    ]
+    for copy in copies:
+        copy.start()
+    for copy in copies:
+        copy.wait()
+
+
+def join_call(blocks):
+    return pl.pallas_call(
+        join_kernel,
+        out_shape=jax.ShapeDtypeStruct((len(blocks),) + blocks[0].shape, blocks[0].dtype),
+        in_specs=[pl.BlockSpec(memory_space=pl.ANY) for _ in blocks],
+        out_specs=pl.BlockSpec(memory_space=pl.ANY),
+        scratch_shapes=[pltpu.SemaphoreType.DMA((len(blocks),))],
+        compiler_params=pltpu.CompilerParams(vmem_limit_bytes=VMEM),
+        name="join",
+    )(*blocks)
+
+
 def from_before(x, axis, k):
     if k == 0:
         return x
@@ -608,9 +631,10 @@
         deep_bias,
         out_weight.reshape(1, WIDTH),
     )
-    mine = jnp.stack([from_before(grads[k], "rep", k) for k in range(REPS)])
+    mine = join_call([from_before(grads[k], "rep", k) for k in range(REPS)])
     mine, kept, given = lax.optimization_barrier((mine, kept, given))
     all_grads = lax.all_gather(mine, "shard", axis=0)
+    all_grads, logits = lax.optimization_barrier((all_grads, logits.reshape(SAMPLES)))
     other = lax.ppermute(given, "shard", [(i, i ^ 1) for i in range(OWNERS)])
     half = (kept.astype(F32) + other.astype(F32)).astype(BF)
     quarter = summed(exchange(half, "rep"))
@@ -638,7 +662,7 @@
     near, far = places[: 3 * PAIR], places[3 * PAIR :]
     row_grad = finish_call(near, [part, before, after])
     row_grad = finish_call(far, across, row_grad)
-    return (row_grad, first_grad, logits.reshape(SAMPLES))
+    return (row_grad, first_grad, logits)
 
 
 def solution(mesh):

time: 258 us -> 267 us (1.035)
  the two profiles are of different devices: /device:TPU:70 before, /device:TPU:71 now
where the time goes in v1:
time: 267 us
  Pallas kernels  107 us (40%)
  waiting for transfers between devices  56.7 us (21%)
  blocking collectives  39.6 us (15%)
  starting transfers between devices  34.1 us (13%)
  between operations  14.3 us (5%)
  other arithmetic  9.39 us (4%)
  local copies, waits for them, and re-layouts  6.4 us (2%)
    pallas_call x1, Pallas kernels, scatter_call(): pl.pallas_call(scatter_kernel, out_shape=jax.ShapeDtypeStruct((rows, EMB)...  44.5 us
    ppermute x13, waiting for transfers between devices, from_before(): return lax.ppermute(x, axis, [(i, (i + k) % n) for i in range(n)])  22.6 us
    pallas_call x2, Pallas kernels, gather_call(): pl.pallas_call(functools.partial(gather_kernel, offset), out_shape=jax.Sh...  21.4 us
    all_to_all x2, waiting for transfers between devices, exchange(): return lax.all_to_all(x, axis, split_axis=0, concat_axis=0, tiled=True)  18.6 us
    all_to_all x1, blocking collectives, exchange(): return lax.all_to_all(x, axis, split_axis=0, concat_axis=0, tiled=True)  17.6 us
    ppermute x13, starting transfers between devices, from_before(): return lax.ppermute(x, axis, [(i, (i + k) % n) for i in range(n)])  16.6 us
    pallas_call x1, Pallas kernels, tower_call(): pl.pallas_call(functools.partial(tower_kernel, CAP - got.shape[1]), grid=...  15.5 us
    all_to_all x2, starting transfers between devices, exchange(): return lax.all_to_all(x, axis, split_axis=0, concat_axis=0, tiled=True)  15.2 us
  transfers between devices with their start and end apart: 18, of which 11 were waited for; matrix products, arithmetic and copies ran while one was open for 5% of the time, Pallas kernels for 24%

profile of v1, /device:TPU:71, one launch (start us, length us, event | category | flops | bytes accessed | tf_op | source)
XLA Modules:
  0.0 267.4 jit_solution(8272289152456419967)
XLA Ops:
  7.2 9.1 %index.1 = (s32[32,512]{1,0:T(8,128)}, s32[32,4,128]{2,1,0:T(4,128)}) custom-call(s32[1,8192]{1,0:T(1,128)} %ids_in.1, s32[1,8192]{1,0:T(1,128)} %bitcast.30, s32[1,1024]{1,0:T(1,128)} %len_in.1, s32[8,32]{1,0:T(8,128)} %bitcast.31), custom_call_target="tpu_custom_call" | custom-call | tf_op jit(solution)/shard_map/index/pallas_call | solution.py:146
  16.3 11.6 %all_to_all.25 = s32[32,4,128]{2,1,0:T(4,128)S(1)} all-to-all(s32[32,4,128]{2,1,0:T(4,128)} %get-tuple-element.27), channel_id=1, replica_groups=mesh['rep'=4,'shard'=32] {'shard'}, dimensions={0} | all-to-all | bytes 131072 | tf_op jit(solution)/shard_map/all_to_all | solution.py:568
  28.5 6.6 %gather.9 = bf16[32,128,128]{2,1,0:T(8,128)(2,1)} custom-call(s32[16384]{0:T(1024)} %bitcast.25, bf16[8192,128]{1,0:T(8,128)(2,1)} %table_ref.3), custom_call_target="tpu_custom_call" | custom-call | tf_op jit(solution)/shard_map/gather/pallas_call | solution.py:187
  35.1 7.8 %all-to-all-start.2 = ((bf16[32,128,128]{2,1,0:T(8,128)(2,1)}), bf16[32,128,128]{2,1,0:T(8,128)(2,1)S(1)}, u32[]{:S(2)}, u32[]{:S(2)}) async-start(bf16[32,128,128]{2,1,0:T(8,128)(2,1)} %gather.9), calls=%async_computation.2 | async-start | bytes 2097152 | tf_op jit(solution)/shard_map/all_to_all | solution.py:572
  42.9 14.8 %gather.8 = bf16[32,384,128]{2,1,0:T(8,128)(2,1)} custom-call(s32[16384]{0:T(1024)} %bitcast.26, bf16[8192,128]{1,0:T(8,128)(2,1)} %table_ref.3), custom_call_target="tpu_custom_call" | custom-call | tf_op jit(solution)/shard_map/gather/pallas_call | solution.py:187
  58.7 7.4 %all-to-all-start.1 = ((bf16[32,384,128]{2,1,0:T(8,128)(2,1)}), bf16[32,384,128]{2,1,0:T(8,128)(2,1)}, u32[]{:S(2)}, u32[]{:S(2)}) async-start(bf16[32,384,128]{2,1,0:T(8,128)(2,1)} %gather.8), calls=%async_computation.1 | async-start | bytes 6291456 | tf_op jit(solution)/shard_map/all_to_all | solution.py:572
  68.0 2.8 %collective-permute-start.2 = (s32[32,4,128]{2,1,0:T(4,128)S(1)}, s32[32,4,128]{2,1,0:T(4,128)S(1)}, u32[]{:S(2)}, u32[]{:S(2)}) collective-permute-start(s32[32,4,128]{2,1,0:T(4,128)S(1)} %all_to_all.25), channel_id=1, source_target_pairs={{0,96},{32,0},{64,32},{96,64},{1,97},{33,1},{65,33},{97,65},{2,98}... | collective-permute-start | bytes 196616 | tf_op jit(solution)/shard_map/ppermute | solution.py:534
  72.4 3.3 %collective-permute-done.1 = s32[32,4,128]{2,1,0:T(4,128)S(1)} collective-permute-done((s32[32,4,128]{2,1,0:T(4,128)S(1)}, s32[32,4,128]{2,1,0:T(4,128)S(1)}, u32[]{:S(2)}, u32[]{:S(2)}) %collective-permute-start.1) | collective-permute-done | bytes 65568 | tf_op jit(solution)/shard_map/ppermute | solution.py:534
  81.2 3.5 %pool.1.earlier_ref = f32[128,1024]{1,0:T(8,128)} custom-call(bf16[32,128,128]{2,1,0:T(8,128)(2,1)} %copy-done.1, s32[32,512]{1,0:T(8,128)} %get-tuple-element.31.packed_ref), custom_call_target="tpu_custom_call" | custom-call | tf_op jit(solution)/shard_map/pool/pallas_call | solution.py:236
  84.7 18.6 %all-to-all-done.1.got_ref = bf16[32,384,128]{2,1,0:T(8,128)(2,1)} async-done(((bf16[32,384,128]{2,1,0:T(8,128)(2,1)}), bf16[32,384,128]{2,1,0:T(8,128)(2,1)}, u32[]{:S(2)}, u32[]{:S(2)}) %all-to-all-start.1) | async-done | bytes 3145760 | tf_op jit(solution)/shard_map/all_to_all | solution.py:572
  103.3 15.5 %tower.1 = (f32[128,1]{1,0:T(8,128)}, bf16[4,128,1024]{2,1,0:T(8,128)(2,1)}, bf16[4,128,1024]{2,1,0:T(8,128)(2,1)}, bf16[128,256]{1,0:T(8,128)(2,1)}, bf16[128,2...) custom-call(s32[2]{0:T(128)} %pad_add_fusion.1.me_ref, ...), custom_call_target="tpu_custom_call" | custom-call | tf_op jit(solution)/shard_map/tower/pallas_call | solution.py:356
  120.1 2.6 collective-permute-start.4
  127.1 9.1 %join.1 = bf16[4,128,256]{2,1,0:T(8,128)(2,1)} custom-call(bf16[128,256]{1,0:T(8,128)(2,1)} %get-tuple-element.39.refs_0_, bf16[128,256]{1,0:T(8,128)(2,1)} %copy-done.3, bf16[128,256]{1,0:T(8,128)(2,1)} %copy-done.4, bf16[128,256]{1,0:T(8,128)(2,1)} %copy-done.5), custom_call_target="tpu_custom_call" | custom-call | tf_op jit(solution)/shard_map/join/pallas_call | solution.py:519
  136.3 2.2 collective-permute-start.10
  138.5 2.5 collective-permute-done.10
  142.5 17.6 %all_to_all.26 = bf16[4,128,1024]{2,1,0:T(8,128)(2,1)S(1)} all-to-all(bf16[4,128,1024]{2,1,0:T(8,128)(2,1)S(1)} %add_convert_fusion), channel_id=1, replica_groups=mesh['rep'=4,'shard'=32] {'rep'}, dimensions={0} | all-to-all | bytes 2097152 | tf_op jit(solution)/shard_map/all_to_all | solution.py:572
  160.3 10.5 %all_to_all.27 = bf16[16,8,1024]{2,1,0:T(8,128)(2,1)S(1)} all-to-all(bf16[16,8,1024]{2,1,0:T(8,128)(2,1)S(1)} %bitcast.23), channel_id=1, replica_groups={{0,2,4,6,8,10,12,14,16,18,20,22,24,26,28,30},{1,3,5,7,9,11,13,15,17,19,..., dimensions={0} | all-to-all | bytes 524288 | tf_op jit(solution)/shard_map/all_to_all | solution.py:642
  178.4 13.0 %all-gather.6.cloned.1.call-done = bf16[128,128,256]{2,1,0:T(8,128)(2,1)} async-done(((bf16[4,128,256]{2,1,0:T(8,128)(2,1)}), bf16[128,128,256]{2,1,0:T(8,128)(2,1)}) %all-gather.6.cloned.1.call-update) | async-done | bytes 8388624 | tf_op jit(solution)/shard_map/all_gather | solution.py:636
  191.4 44.5 %scatter.1 = bf16[2048,128]{1,0:T(8,128)(2,1)} custom-call(s32[128]{0:T(128)} %add.93.first_ref, s32[128]{0:T(128)} %reshape.89.trips_ref, s32[73728]{0:T(1024)} %reshape.81.word_ref, bf16[32,4,128,256]{3,2,1,0:T(8,128)(2,1)} %bitcast.22), custom_call_target="tpu_custom_call" | custom-call | tf_op jit(solution)/shard_map/scatter/pallas_call | solution.py:447
  235.9 2.7 collective-permute-start.8
  238.6 10.8 %collective-permute-done.6.refs_1_ = bf16[2,1024,128]{2,1,0:T(8,128)(2,1)S(1)} collective-permute-done((bf16[2,1024,128]{2,1,0:T(8,128)(2,1)}, bf16[2,1024,128]{2,1,0:T(8,128)(2,1)S(1)}, u32[]{:S(2)}, u32[]{:S(2)}) %collective-permute-start.6) | collective-permute-done | bytes 524320 | tf_op jit(solution)/shard_map/ppermute | solution.py:534
  249.6 2.9 %collective-permute-start.9 = (bf16[1,1024,128]{2,1,0:T(8,128)(2,1)S(1)}, bf16[1,1024,128]{2,1,0:T(8,128)(2,1)S(1)}, u32[]{:S(2)}, u32[]{:S(2)}) collective-permute-start(bf16[1,1024,128]{2,1,0:T(8,128)(2,1)S(1)} %slice.19), channel_id=1, source_target_pairs={{0,96},{32,0},{64,32},{96,64},{1,97},{33,1},{65,33},{97,65},{2,98}... | collective-permute-start | bytes 786440 | tf_op jit(solution)/shard_map/ppermute | solution.py:534
  252.5 4.1 %convert_element_type.27 = f32[1024,1024]{1,0:T(8,128)} convert(bf16[1024,1024]{1,0:T(8,128)(2,1)} %all-gather.4.cloned.1.call-done) | non-fusion elementwise | flops 1048576 | bytes 6291456 | tf_op jit(solution)/shard_map/convert_element_type | solution.py:653
  256.7 2.3 finish.2.refs_2_
  (77 shorter events, 27.4 us)
Async XLA Ops:
  35.1 22.6 %all-to-all-start.2 = ((bf16[32,128,128]{2,1,0:T(8,128)(2,1)}), bf16[32,128,128]{2,1,0:T(8,128)(2,1)S(1)}, u32[]{:S(2)}, u32[]{:S(2)}) async-start(bf16[32,128,128]{2,1,0:T(8,128)(2,1)} %gather.9), calls=%async_computation.2 | async-start | bytes 2097152 | tf_op jit(solution)/shard_map/all_to_all | solution.py:572
  57.7 8.5 %copy-start.6 = (s32[32,8]{0,1:T(8,128)S(1)}, s32[32,8]{0,1:T(8,128)}, u32[]{:S(2)}) copy-start(s32[32,8]{0,1:T(8,128)} %param.17) | copy-start | bytes 3076
  57.7 8.7 %copy-start.8 = (s32[4]{0:T(128)S(1)}, s32[4]{0:T(128)}, u32[]{:S(2)}) copy-start(s32[4]{0:T(128)} %constant.94) | copy-start | bytes 52
  57.7 8.9 %copy-start.7 = (s32[128]{0:T(128)S(1)}, s32[128]{0:T(128)}, u32[]{:S(2)}) copy-start(s32[128]{0:T(128)} %param.18) | copy-start | bytes 1540
  58.7 44.6 %all-to-all-start.1 = ((bf16[32,384,128]{2,1,0:T(8,128)(2,1)}), bf16[32,384,128]{2,1,0:T(8,128)(2,1)}, u32[]{:S(2)}, u32[]{:S(2)}) async-start(bf16[32,384,128]{2,1,0:T(8,128)(2,1)} %gather.8), calls=%async_computation.1 | async-start | bytes 6291456 | tf_op jit(solution)/shard_map/all_to_all | solution.py:572
  66.1 125.3 %all-gather.6.cloned.1.call-start = ((), (), s32[]{:S(2)}) async-start(), calls=%async_computation.6 | async-start | bytes 8650752 | tf_op jit(solution)/shard_map/all_gather | solution.py:636
  68.0 4.5 %collective-permute-start.2 = (s32[32,4,128]{2,1,0:T(4,128)S(1)}, s32[32,4,128]{2,1,0:T(4,128)S(1)}, u32[]{:S(2)}, u32[]{:S(2)}) collective-permute-start(s32[32,4,128]{2,1,0:T(4,128)S(1)} %all_to_all.25), channel_id=1, source_target_pairs={{0,96},{32,0},{64,32},{96,64},{1,97},{33,1},{65,33},{97,65},{2,98}... | collective-permute-start | bytes 196616 | tf_op jit(solution)/shard_map/ppermute | solution.py:534
  70.8 5.0 %collective-permute-start.1 = (s32[32,4,128]{2,1,0:T(4,128)S(1)}, s32[32,4,128]{2,1,0:T(4,128)S(1)}, u32[]{:S(2)}, u32[]{:S(2)}) collective-permute-start(s32[32,4,128]{2,1,0:T(4,128)S(1)} %all_to_all.25), channel_id=1, source_target_pairs={{0,64},{32,96},{64,0},{96,32},{1,65},{33,97},{65,1},{97,33},{2,66}... | collective-permute-start | bytes 196616 | tf_op jit(solution)/shard_map/ppermute | solution.py:534
  71.1 6.2 %collective-permute-start = (s32[32,4,128]{2,1,0:T(4,128)S(1)}, s32[32,4,128]{2,1,0:T(4,128)S(1)}, u32[]{:S(2)}, u32[]{:S(2)}) collective-permute-start(s32[32,4,128]{2,1,0:T(4,128)S(1)} %all_to_all.25), channel_id=1, source_target_pairs={{0,32},{32,64},{64,96},{96,0},{1,33},{33,65},{65,97},{97,1},{2,34}... | collective-permute-start | bytes 196616 | tf_op jit(solution)/shard_map/ppermute | solution.py:534
  118.7 5.1 %collective-permute-start.3 = (bf16[128,256]{1,0:T(8,128)(2,1)}, bf16[128,256]{1,0:T(8,128)(2,1)S(1)}, u32[]{:S(2)}, u32[]{:S(2)}) collective-permute-start(bf16[128,256]{1,0:T(8,128)(2,1)} %get-tuple-element.40), channel_id=1, source_target_pairs={{0,32},{32,64},{64,96},{96,0},{1,33},{33,65},{65,97},{97,1},{2,34}... | collective-permute-start | bytes 196616 | tf_op jit(solution)/shard_map/ppermute | solution.py:534
  120.1 5.3 %collective-permute-start.4 = (bf16[128,256]{1,0:T(8,128)(2,1)}, bf16[128,256]{1,0:T(8,128)(2,1)S(1)}, u32[]{:S(2)}, u32[]{:S(2)}) collective-permute-start(bf16[128,256]{1,0:T(8,128)(2,1)} %get-tuple-element.41), channel_id=1, source_target_pairs={{0,64},{32,96},{64,0},{96,32},{1,65},{33,97},{65,1},{97,33},{2,66}... | collective-permute-start | bytes 196616 | tf_op jit(solution)/shard_map/ppermute | solution.py:534
  122.7 3.8 %collective-permute-start.5 = (bf16[128,256]{1,0:T(8,128)(2,1)}, bf16[128,256]{1,0:T(8,128)(2,1)S(1)}, u32[]{:S(2)}, u32[]{:S(2)}) collective-permute-start(bf16[128,256]{1,0:T(8,128)(2,1)} %get-tuple-element.42), channel_id=1, source_target_pairs={{0,96},{32,0},{64,32},{96,64},{1,97},{33,1},{65,33},{97,65},{2,98}... | collective-permute-start | bytes 196616 | tf_op jit(solution)/shard_map/ppermute | solution.py:534
  123.8 2.7 %copy-start.3 = (bf16[128,256]{1,0:T(8,128)(2,1)}, bf16[128,256]{1,0:T(8,128)(2,1)S(1)}, u32[]{:S(2)}) copy-start(bf16[128,256]{1,0:T(8,128)(2,1)S(1)} %collective-permute-done.3.refs_1_) | copy-start | bytes 196612
  136.2 41.5 %copy-start.2 = (f32[128,1]{1,0:T(8,128)S(1)}, f32[128,1]{1,0:T(8,128)}, u32[]{:S(2)}) copy-start(f32[128,1]{1,0:T(8,128)} %get-tuple-element.46) | copy-start | bytes 1540
  136.2 116.3 %all-gather.4.cloned.1.call-start = ((), (), s32[]{:S(2)}) async-start(), calls=%async_computation.5 | async-start | bytes 2162688 | tf_op jit(solution)/shard_map/all_gather | solution.py:651
  136.3 4.7 %collective-permute-start.10 = (bf16[4,128,1024]{2,1,0:T(8,128)(2,1)}, bf16[4,128,1024]{2,1,0:T(8,128)(2,1)S(1)}, u32[]{:S(2)}, u32[]{:S(2)}) collective-permute-start(bf16[4,128,1024]{2,1,0:T(8,128)(2,1)} %get-tuple-element.49), channel_id=1, source_target_pairs={{0,1},{1,0},{2,3},{3,2},{4,5},{5,4},{6,7},{7,6},{8,9},{9,8},{10,11... | collective-permute-start | bytes 3145736 | tf_op jit(solution)/shard_map/ppermute | solution.py:638
  170.8 3.1 %collective-permute-start.11 = (bf16[8,1024]{1,0:T(8,128)(2,1)S(1)}, bf16[8,1024]{1,0:T(8,128)(2,1)S(1)}, u32[]{:S(2)}, u32[]{:S(2)}) collective-permute-start(bf16[8,1024]{1,0:T(8,128)(2,1)S(1)} %reduce_sum.45), channel_id=1, source_target_pairs={{0,96},{32,0},{64,32},{96,64},{1,97},{33,1},{65,33},{97,65},{2,98}... | collective-permute-start | bytes 49160 | tf_op jit(solution)/shard_map/ppermute | solution.py:534
  171.6 4.1 %collective-permute-start.12 = (bf16[8,1024]{1,0:T(8,128)(2,1)S(1)}, bf16[8,1024]{1,0:T(8,128)(2,1)S(1)}, u32[]{:S(2)}, u32[]{:S(2)}) collective-permute-start(bf16[8,1024]{1,0:T(8,128)(2,1)S(1)} %reduce_sum.45), channel_id=1, source_target_pairs={{0,64},{32,96},{64,0},{96,32},{1,65},{33,97},{65,1},{97,33},{2,66}... | collective-permute-start | bytes 49160 | tf_op jit(solution)/shard_map/ppermute | solution.py:534
  172.9 4.2 %collective-permute-start.13 = (bf16[8,1024]{1,0:T(8,128)(2,1)S(1)}, bf16[8,1024]{1,0:T(8,128)(2,1)S(1)}, u32[]{:S(2)}, u32[]{:S(2)}) collective-permute-start(bf16[8,1024]{1,0:T(8,128)(2,1)S(1)} %reduce_sum.45), channel_id=1, source_target_pairs={{0,32},{32,64},{64,96},{96,0},{1,33},{33,65},{65,97},{97,1},{2,34}... | collective-permute-start | bytes 49160 | tf_op jit(solution)/shard_map/ppermute | solution.py:534
  235.9 13.5 %collective-permute-start.6 = (bf16[2,1024,128]{2,1,0:T(8,128)(2,1)}, bf16[2,1024,128]{2,1,0:T(8,128)(2,1)S(1)}, u32[]{:S(2)}, u32[]{:S(2)}) collective-permute-start(bf16[2,1024,128]{2,1,0:T(8,128)(2,1)} %bitcast.18), channel_id=1, source_target_pairs={{0,32},{32,64},{64,96},{96,0},{1,33},{33,65},{65,97},{97,1},{2,34}... | collective-permute-start | bytes 1572872 | tf_op jit(solution)/shard_map/ppermute | solution.py:534
  235.9 13.6 %collective-permute-start.8 = (bf16[2,1024,128]{2,1,0:T(8,128)(2,1)}, bf16[2,1024,128]{2,1,0:T(8,128)(2,1)S(1)}, u32[]{:S(2)}, u32[]{:S(2)}) collective-permute-start(bf16[2,1024,128]{2,1,0:T(8,128)(2,1)} %bitcast.19), channel_id=1, source_target_pairs={{0,96},{32,0},{64,32},{96,64},{1,97},{33,1},{65,33},{97,65},{2,98}... | collective-permute-start | bytes 1572872 | tf_op jit(solution)/shard_map/ppermute | solution.py:534
  249.4 9.5 %collective-permute-start.7 = (bf16[1,1024,128]{2,1,0:T(8,128)(2,1)S(1)}, bf16[1,1024,128]{2,1,0:T(8,128)(2,1)S(1)}, u32[]{:S(2)}, u32[]{:S(2)}) collective-permute-start(bf16[1,1024,128]{2,1,0:T(8,128)(2,1)S(1)} %slice.18), channel_id=1, source_target_pairs={{0,32},{32,64},{64,96},{96,0},{1,33},{33,65},{65,97},{97,1},{2,34}... | collective-permute-start | bytes 786440 | tf_op jit(solution)/shard_map/ppermute | solution.py:534
  249.6 9.4 %collective-permute-start.9 = (bf16[1,1024,128]{2,1,0:T(8,128)(2,1)S(1)}, bf16[1,1024,128]{2,1,0:T(8,128)(2,1)S(1)}, u32[]{:S(2)}, u32[]{:S(2)}) collective-permute-start(bf16[1,1024,128]{2,1,0:T(8,128)(2,1)S(1)} %slice.19), channel_id=1, source_target_pairs={{0,96},{32,0},{64,32},{96,64},{1,97},{33,1},{65,33},{97,65},{2,98}... | collective-permute-start | bytes 786440 | tf_op jit(solution)/shard_map/ppermute | solution.py:534
  252.5 4.1 %copy-start = (bf16[2048,128]{1,0:T(8,128)(2,1)S(1)}, bf16[2048,128]{1,0:T(8,128)(2,1)}, u32[]{:S(2)}) copy-start(bf16[2048,128]{1,0:T(8,128)(2,1)} %scatter.1) | copy-start | bytes 1572868
  (3 other events, 2.7 us)
Sparse Core Ops, SparseCore 0:
  136.4 55.0 all-gather.5
  194.3 41.8 all-gather.3
